TPU v7x, 256 devices: a whole 4x4x8 slice. The times are simulated.
256 devices in a mesh: depth: 16 (over z, core), row: 4 (over x), col: 4 (over y).
Axes of the slice: x: 4, y: 4, z: 8, core: 2. Of those that a mesh axis runs over, the one named last changes fastest.
Arguments:
- tile_left: bfloat16 [16, 16, 64, 1024], P('row', 'col'), may hold values from -6 to 6
- tile_right: bfloat16 [16, 16, 64, 1024], P('row', 'col'), may hold values from -6 to 6
- row_left: bfloat16 [16, 64, 64, 1024], P('row', 'depth', None, 'col'), may hold values from -6 to 6
- row_right: bfloat16 [16, 64, 64, 1024], P('row', 'depth', None, 'col'), may hold values from -0.1875 to 0.1875
- col_left: bfloat16 [16, 64, 64, 1024], P('col', 'depth', None, 'row'), may hold values from -6 to 6
- col_right: bfloat16 [16, 64, 64, 1024], P('col', 'depth', None, 'row'), may hold values from -0.1875 to 0.1875
- row_mask: int32 [16, 64], P('row', 'depth'), may hold values 0 or 1
- col_mask: int32 [16, 64], P('col', 'depth'), may hold values 0 or 1
- sketch: bfloat16 [64, 1024], replicated, may hold values from -1 to 1
Outputs:
- new_left: float32 [16, 16, 64, 1024], P('row', 'col', 'depth')
- new_right: float32 [16, 16, 64, 1024], P('row', 'col', 'depth')
All inputs are finite; a program needn't handle non-finite values. No bound on the sum of `row_mask` or of `col_mask` on one device may be relied on, other than what follows from the above.
Results may differ from a plain program's by a relative error of at most 0.0003.
Values may be sent and summed in bfloat16 or wider, within the bound.
A program may use at most 64 MiB of HBM per device.

v0:
```python
import math

import jax
import jax.numpy as jnp
from jax import lax
from jax.sharding import PartitionSpec as P

NB = 1024
K = 64


exact_mode = lax.Precision.HIGHEST


def orthonormalize(sketched):
    for repeat in range(2):
        gram_mat = jnp.einsum("ijtn,ijsn->ijts", sketched, sketched, precision=exact_mode)
        factor = jnp.linalg.cholesky(gram_mat)
        sketched = jax.scipy.linalg.solve_triangular(factor, sketched, lower=True)
    return sketched


def on_device(
    tile_left, tile_right, row_left, row_right, col_left, col_right, row_mask, col_mask, sketch
):
    row_full_left, row_full_right = (
        lax.all_gather(row_left, "col", axis=3, tiled=True),
        lax.all_gather(row_right, "col", axis=3, tiled=True),
    )
    col_full_left, col_full_right = (
        lax.all_gather(col_left, "row", axis=3, tiled=True),
        lax.all_gather(col_right, "row", axis=3, tiled=True),
    )
    weight_table = (
        row_mask.astype(jnp.float32)[:, None, :] * col_mask.astype(jnp.float32)[None, :, :]
    )
    coupling = jnp.einsum(
        "ikrn,jksn->ijkrs", row_full_right, col_full_right, preferred_element_type=jnp.float32
    )
    coupling = coupling * weight_table[:, :, :, None, None]
    col_sketch = jnp.einsum(
        "jksn,tn->jkst", col_full_left, sketch, preferred_element_type=jnp.float32
    )
    mixing = jnp.einsum("ijkrs,jkst->ijkrt", coupling, col_sketch, precision=exact_mode)
    partial_sketch = -jnp.einsum(
        "ijkrt,ikrn->ijtn",
        mixing,
        row_full_left,
        precision=exact_mode,
        preferred_element_type=jnp.float32,
    )
    sketch_right = jnp.einsum(
        "ijrn,tn->ijrt", tile_right, sketch, preferred_element_type=jnp.float32
    )
    summed = lax.psum(partial_sketch, "depth")
    sketched = summed + jnp.einsum(
        "ijrt,ijrn->ijtn",
        sketch_right,
        tile_left,
        precision=exact_mode,
        preferred_element_type=jnp.float32,
    )
    basis = orthonormalize(sketched)
    rank_rows = K // lax.axis_size("depth")
    rank_offset = lax.axis_index("depth") * rank_rows
    basis_mine = lax.dynamic_slice_in_dim(basis, rank_offset, rank_rows, 2)
    basis_row = jnp.einsum(
        "ijtn,ikrn->ijktr",
        basis,
        row_full_left,
        precision=exact_mode,
        preferred_element_type=jnp.float32,
    )
    projected = jnp.einsum("ijktr,ijkrs->ijkts", basis_row, coupling, precision=exact_mode)
    right_part = -jnp.einsum(
        "ijkts,jksn->ijtn",
        projected,
        col_full_left,
        precision=exact_mode,
        preferred_element_type=jnp.float32,
    )
    right_share = lax.psum_scatter(right_part, "depth", scatter_dimension=2, tiled=True)
    own_part = jnp.einsum(
        "ijtn,ijrn->ijtr",
        basis_mine,
        tile_left,
        precision=exact_mode,
        preferred_element_type=jnp.float32,
    )
    right_share = right_share + jnp.einsum(
        "ijtr,ijrn->ijtn",
        own_part,
        tile_right,
        precision=exact_mode,
        preferred_element_type=jnp.float32,
    )
    return (basis_mine * math.sqrt(NB), right_share / math.sqrt(NB))


def solution(mesh):
    in_specs = (
        P("row", "col", None, None),
        P("row", "col", None, None),
        P("row", "depth", None, "col"),
        P("row", "depth", None, "col"),
        P("col", "depth", None, "row"),
        P("col", "depth", None, "row"),
        P("row", "depth"),
        P("col", "depth"),
        P(),
    )
    out_specs = (P("row", "col", "depth", None), P("row", "col", "depth", None))
    return jax.shard_map(
        on_device, mesh=mesh, in_specs=in_specs, out_specs=out_specs, check_vma=False
    )
```

profile of v0, /device:TPU:1, one launch (start us, length us, event | category | flops | bytes accessed | tf_op | source)
XLA Modules:
  0.0 817.5 jit_solution(13428077968273301027)
XLA Ops:
  7.2 0.0 copy-start
  7.2 0.0 all-gather.5.cloned.1.call-start
  7.3 0.7 all-gather.5.cloned.1.call-update
  8.0 0.0 all-gather.7.cloned.1.call-start
  8.0 1.9 copy.30
  9.9 0.0 all-gather.7.cloned.1.call-update
  9.9 0.0 all-gather.9.cloned.1.call-start
  10.0 0.8 copy.31
  10.8 0.0 all-gather.9.cloned.1.call-update
  10.8 0.0 all-gather.11.cloned.1.call-start
  10.9 0.5 all-gather.11.cloned.1.call-update
  11.4 0.0 all-reduce.4.cloned.1.call-start
  11.5 0.1 copy.32
  11.6 0.0 copy-done.11
  11.6 0.1 copy.33
  11.7 0.1 broadcast_multiply_fusion
  11.8 38.1 %all-gather.5.cloned.1.call-done = bf16[4,4,64,1024]{3,2,1,0:T(8,128)(2,1)} async-done(((bf16[4,4,64,256]{3,2,1,0:T(8,128)(2,1)}), bf16[4,4,64,1024]{3,2,1,0:T(8,128)(2,1)}) %all-gather.5.cloned.1.call-update) | async-done | bytes 2097168 | tf_op jit(solution)/shard_map/all_gather | solution.py:31
  49.8 2.7 convolution_bitcast_fusion
  52.5 37.2 %all-gather.7.cloned.1.call-done = bf16[4,4,64,1024]{3,2,0,1:T(8,128)(2,1)} async-done(((bf16[4,4,64,256]{3,2,0,1:T(8,128)(2,1)}), bf16[4,4,64,1024]{3,2,0,1:T(8,128)(2,1)}) %all-gather.7.cloned.1.call-update) | async-done | bytes 2097168 | tf_op jit(solution)/shard_map/all_gather | solution.py:32
  89.7 39.9 %all-gather.9.cloned.1.call-done = bf16[4,4,64,1024]{3,2,0,1:T(8,128)(2,1)} async-done(((bf16[4,4,64,256]{3,2,0,1:T(8,128)(2,1)}), bf16[4,4,64,1024]{3,2,0,1:T(8,128)(2,1)}) %all-gather.9.cloned.1.call-update) | async-done | bytes 2097168 | tf_op jit(solution)/shard_map/all_gather | solution.py:28
  129.6 3.5 bitcast_multiply_fusion
  133.1 1.3 copy-done.5
  134.5 3.1 fusion.12
  137.6 31.8 %all-gather.11.cloned.1.call-done = bf16[4,4,64,1024]{3,2,1,0:T(8,128)(2,1)} async-done(((bf16[4,4,64,256]{3,2,1,0:T(8,128)(2,1)}), bf16[4,4,64,1024]{3,2,1,0:T(8,128)(2,1)}) %all-gather.11.cloned.1.call-update) | async-done | bytes 2097168 | tf_op jit(solution)/shard_map/all_gather | solution.py:27
  169.4 6.1 bitcast_negate_fusion.1
  175.5 0.0 all-reduce.4.cloned.1.call-update
  175.6 0.2 all-reduce.6.cloned.1.call-start
  175.8 2.7 fusion.33
  178.5 120.0 %all-reduce.4.cloned.1.call-done = f32[4,4,64,1024]{3,2,1,0:T(8,128)} async-done(((f32[4,4,64,1024]{3,2,1,0:T(8,128)}), f32[4,4,64,1024]{3,2,1,0:T(8,128)}) %all-reduce.4.cloned.1.call-update) | async-done | bytes 4194320 | tf_op jit(solution)/shard_map/psum | solution.py:55
  298.5 4.1 convolution_add_fusion
  302.7 1.9 copy-done.2
  304.6 4.0 fusion.37
  308.6 0.2 copy.37
  308.8 0.9 fusion.30
  309.7 94.5 %custom-call.8 = f32[4,4,64,64]{3,2,1,0:T(8,128)S(1)} custom-call(f32[4,4,64,64]{3,2,1,0:T(8,128)} %fusion.30), custom_call_target="Cholesky" | custom-call | tf_op jit(solution)/shard_map/jit(cholesky)/cholesky | solution.py:18
  404.2 0.1 select_reduce_fusion.1
  404.3 0.1 compare_reduce_fusion.1
  404.4 0.1 select_bitcast_fusion.1
  404.6 78.6 %custom-call.9 = f32[4,4,1,64,64]{3,4,2,1,0:T(8,128)S(1)} custom-call(f32[4,4,1,64,64]{4,3,2,1,0:T(8,128)S(1)} %select_bitcast_fusion.1), custom_call_target="InvertDiagBlocksLowerTriangular" | custom-call | tf_op jit(solution)/shard_map/jit(_solve_triangular)/vmap(vmap())/triangular_solve | solution.py:19
  483.2 5.5 fusion.28
  488.7 0.0 copy-start.1
  488.7 1.9 copy-done.1
  490.7 4.0 fusion.38
  494.7 0.2 copy.39
  494.9 0.9 fusion.27
  495.7 94.5 %custom-call.10 = f32[4,4,64,64]{3,2,1,0:T(8,128)S(1)} custom-call(f32[4,4,64,64]{3,2,1,0:T(8,128)} %fusion.27), custom_call_target="Cholesky" | custom-call | tf_op jit(solution)/shard_map/jit(cholesky)/cholesky | solution.py:18
  590.2 0.1 select_reduce_fusion
  590.3 0.1 compare_reduce_fusion
  590.5 0.1 select_bitcast_fusion
  590.6 78.6 %custom-call.11 = f32[4,4,1,64,64]{3,4,2,1,0:T(8,128)S(1)} custom-call(f32[4,4,1,64,64]{4,3,2,1,0:T(8,128)S(1)} %select_bitcast_fusion), custom_call_target="InvertDiagBlocksLowerTriangular" | custom-call | tf_op jit(solution)/shard_map/jit(_solve_triangular)/vmap(vmap())/triangular_solve | solution.py:19
  669.3 0.0 copy-start.4
  669.3 5.9 fusion.25
  675.2 0.0 copy-done.4
  675.2 0.0 copy-start.3
  675.2 3.5 fusion.19
  678.7 3.5 fusion.7
  682.2 3.5 fusion.2
  685.6 0.0 all-reduce.6.cloned.1.call-update
  685.7 0.6 copy-done.12
  686.3 0.6 dynamic-slice
  687.5 1.8 dynamic-slice_multiply_fusion
  689.4 2.8 fusion.31
  692.1 115.2 %all-reduce.6.cloned.1.call-done = f32[4,4,64,1024]{3,2,0,1:T(8,128)} async-done(((f32[4,4,64,1024]{3,2,0,1:T(8,128)}), f32[4,4,64,1024]{3,2,0,1:T(8,128)}) %all-reduce.6.cloned.1.call-update) | async-done | bytes 4194320
  807.3 3.3 fusion.24
  (20 shorter events, 0.1 us)
Async XLA Ops:
  7.2 291.3 %copy-start = (bf16[4,4,64,1024]{3,2,1,0:T(8,128)(2,1)S(1)}, bf16[4,4,64,1024]{3,2,1,0:T(8,128)(2,1)}, u32[]{:S(2)}) copy-start(bf16[4,4,64,1024]{3,2,1,0:T(8,128)(2,1)} %param.12) | copy-start | bytes 6291460
  7.2 2.8 copy-start.8
  7.2 4.3 copy-start.10
  7.2 4.4 copy-start.11
  7.2 42.6 %copy-start.9 = (bf16[64,1024]{1,0:T(8,128)(2,1)S(1)}, bf16[64,1024]{1,0:T(8,128)(2,1)}, u32[]{:S(2)}) copy-start(bf16[64,1024]{1,0:T(8,128)(2,1)} %param.20) | copy-start | bytes 393220
  7.2 42.6 %all-gather.5.cloned.1.call-start = ((), (), s32[]{:S(2)}) async-start(), calls=%async_computation | async-start | bytes 2621440 | tf_op jit(solution)/shard_map/all_gather | solution.py:31
  8.0 81.8 %all-gather.7.cloned.1.call-start = ((), (), s32[]{:S(2)}) async-start(), calls=%async_computation.1 | async-start | bytes 2621440 | tf_op jit(solution)/shard_map/all_gather | solution.py:32
  9.9 119.7 %all-gather.9.cloned.1.call-start = ((), (), s32[]{:S(2)}) async-start(), calls=%async_computation.2 | async-start | bytes 2621440 | tf_op jit(solution)/shard_map/all_gather | solution.py:28
  10.8 158.5 %all-gather.11.cloned.1.call-start = ((), (), s32[]{:S(2)}) async-start(), calls=%async_computation.3 | async-start | bytes 2621440 | tf_op jit(solution)/shard_map/all_gather | solution.py:27
  11.4 287.1 %all-reduce.4.cloned.1.call-start = ((), (), s32[]{:S(2)}) async-start(), calls=%async_computation.4 | async-start | bytes 8388608 | tf_op jit(solution)/shard_map/psum | solution.py:55
  133.1 1.3 copy-start.5
  175.6 631.8 %all-reduce.6.cloned.1.call-start = ((), (), s32[]{:S(2)}) async-start(), calls=%async_computation.5 | async-start | bytes 8388608
  302.7 1.9 copy-start.2
  488.7 1.9 copy-start.1
  669.3 5.9 copy-start.4
  675.2 3.5 copy-start.3
  675.2 3.5 copy-start.6
  678.7 3.5 copy-start.7
  685.6 0.7 copy-start.12
Sparse Core Ops, SparseCore 0:
  9.9 39.9 all-gather.4
  51.6 38.0 all-gather.6
  91.5 38.0 all-gather.8
  131.3 38.0 all-gather.10
  175.7 122.7 all-reduce.3
  685.8 121.4 all-reduce.5
where the time goes:
time: 818 us; the launch traced here: 817 us
  waiting for transfers between devices  383 us (47%)
  other arithmetic  351 us (43%)
  matrix products  58.2 us (7%)
  between operations  15.1 us (2%)
  local copies, waits for them, and re-layouts  9.8 us (1%)
    another operation x7, other arithmetic, orthonormalize(): factor = jnp.linalg.cholesky(gram_mat)  189 us
    another operation x5, other arithmetic, orthonormalize(): sketched = jax.scipy.linalg.solve_triangular(factor, sketched, lower=True)  158 us
    psum x1, waiting for transfers between devices, on_device(): summed = lax.psum(partial_sketch, 'depth')  120 us
    unnamed x7, waiting for transfers between devices  116 us
    all_gather x1, waiting for transfers between devices, on_device(): lax.all_gather(row_right, 'col', axis=3, tiled=True)  39.9 us
    all_gather x1, waiting for transfers between devices, on_device(): lax.all_gather(col_left, 'row', axis=3, tiled=True)  38.1 us
    all_gather x1, waiting for transfers between devices, on_device(): lax.all_gather(col_right, 'row', axis=3, tiled=True)  37.2 us
    all_gather x1, waiting for transfers between devices, on_device(): lax.all_gather(row_left, 'col', axis=3, tiled=True)  31.8 us
  transfers between devices with their start and end apart: 6, of which 6 were waited for; matrix products, arithmetic and copies ran while one was open for 2% of the time, Pallas kernels for 0%

commit v1 on v0

v1 whole, which is shorter than its diff:
```python
import math

import jax
import jax.numpy as jnp
from jax import lax
from jax.experimental import pallas as pl
from jax.experimental.pallas import tpu as pltpu
from jax.sharding import PartitionSpec as P

NB = 1024
K = 64
MESH = pl.DeviceIdType.MESH
F32 = jnp.float32
BF16 = jnp.bfloat16
HI = lax.Precision.HIGHEST
NZ = 8
NX = 4
CH = NB // NX


def dot_nn(a, b):
    return lax.dot_general(a, b, (((1,), (0,)), ((), ())), preferred_element_type=F32)


def dot_nt(a, b):
    return lax.dot_general(a, b, (((1,), (1,)), ((), ())), preferred_element_type=F32)


def split2(v):
    hi = v.astype(BF16)
    lo = (v - hi.astype(F32)).astype(BF16)
    return hi, lo


def split3(v):
    hi = v.astype(BF16)
    rest = v - hi.astype(F32)
    mid = rest.astype(BF16)
    lo = (rest - mid.astype(F32)).astype(BF16)
    return hi, mid, lo


def kernel(
    rm, cm, tl_in, tr_in, rl_in, rr_in, cl_in, cr_in, sk,
    outl, outr,
    RR, RL, CR, CL, SWR, BDh, BDl, CS, MX, S, SG, RT, RSP, RSM, RQP, RQM,
    TT, TLO, TRO, X, Q, WW, BC, FSL, FSR, FRL, FRR,
    ssem, rsem, lsem,
):
    d = lax.axis_index("depth")
    x = lax.axis_index("row")
    y = lax.axis_index("col")
    c = lax.rem(d, 2)
    o = 1 - c
    z = lax.div(d, 2)

    def zdev(k):
        return (lax.rem(z + k, NZ) * 2 + c, x, y)

    def xdev(k):
        return (d, lax.rem(x + k, NX), y)

    def ydev(k):
        return (d, x, lax.rem(y + k, NX))

    sib = (z * 2 + o, x, y)

    def chunk(base, k):
        return lax.rem(base + k, NX)

    names = {}
    descs = {}

    def send(name, src, dst, dev):
        n = names.setdefault(name, len(names))
        copy = pltpu.make_async_remote_copy(
            src_ref=src, dst_ref=dst, send_sem=ssem.at[n], recv_sem=rsem.at[n],
            device_id=dev, device_id_type=MESH,
        )
        copy.start()
        descs[name] = copy

    def recv(name):
        descs[name].wait_recv()

    barrier = pltpu.get_barrier_semaphore()
    partners = [zdev(k) for k in range(1, NZ)] + [xdev(1), xdev(3), ydev(1), ydev(3), sib]
    for dev in partners:
        pl.semaphore_signal(barrier, inc=1, device_id=dev, device_id_type=MESH)
    tile_i = 2 * c + lax.div(z, 4)
    tile_j = lax.rem(z, 4)
    local = [
        pltpu.make_async_copy(rl_in.at[pl.ds(2 * c, 2)], RL.at[y, :, pl.ds(4 * c, 4)], lsem.at[0]),
        pltpu.make_async_copy(cl_in, CL.at[x, :, pl.ds(4 * c, 4)], lsem.at[1]),
        pltpu.make_async_copy(tl_in.at[tile_i, tile_j], TLO, lsem.at[2]),
        pltpu.make_async_copy(tr_in.at[tile_i, tile_j], TRO, lsem.at[3]),
    ]
    for copy in local:
        copy.start()

    def masked(v, m):
        return (v.astype(F32) * m.astype(F32)).astype(BF16)

    def prep_row(n, _):
        ii, kk = lax.div(n, 4), lax.rem(n, 4)
        RR[y, ii, 4 * c + kk] = masked(rr_in[2 * c + ii, kk], rm[2 * c + ii, kk])
        SWR[ii, kk] = masked(rr_in[2 * o + ii, kk], rm[2 * o + ii, kk])
        return 0

    def prep_col(n, _):
        jj, kk = lax.div(n, 4), lax.rem(n, 4)
        CR[x, jj, 4 * c + kk] = masked(cr_in[jj, kk], cm[jj, kk])
        return 0

    lax.fori_loop(0, 8, prep_row, 0)
    lax.fori_loop(0, 16, prep_col, 0)
    pl.semaphore_wait(barrier, len(partners))

    def grp(buf, b, g):
        return buf.at[b, :, pl.ds(4 * g, 4)]

    def half(buf, a, h, g):
        return buf.at[a, pl.ds(2 * h, 2), pl.ds(4 * g, 4)]

    def row_own(t, buf, src, swap_src):
        send(t + "sw", swap_src, grp(buf, y, c), sib)
        send(t + "y+c", src, grp(buf, y, c), ydev(1))
        send(t + "y-c", src, grp(buf, y, c), ydev(3))

    def row_sib(t, buf):
        recv(t + "sw")
        send(t + "y+o", grp(buf, y, o), grp(buf, y, o), ydev(1))
        send(t + "y-o", grp(buf, y, o), grp(buf, y, o), ydev(3))

    def col_own(t, buf, src):
        send(t + "x+0", src.at[pl.ds(0, 2)], half(buf, x, 0, c), xdev(1))
        send(t + "x-1", src.at[pl.ds(2, 2)], half(buf, x, 1, c), xdev(3))
        send(t + "x+1", src.at[pl.ds(2, 2)], half(buf, x, 1, c), xdev(1))
        send(t + "x-0", src.at[pl.ds(0, 2)], half(buf, x, 0, c), xdev(3))
        send(t + "s", src, buf.at[x, :, pl.ds(4 * c, 4)], sib)

    def col_copy(t, came, buf, a, h):
        recv(t + came)
        send(t + "s" + came, half(buf, a, h, c), half(buf, a, h, c), sib)

    def forward_first(t, rbuf, cbuf):
        recv(t + "y+c")
        send(t + "y+f", grp(rbuf, chunk(y, 3), c), grp(rbuf, chunk(y, 3), c), ydev(1))
        col_copy(t, "x+0", cbuf, chunk(x, 3), 0)
        send(t + "x+f", half(cbuf, chunk(x, 3), 0, c), half(cbuf, chunk(x, 3), 0, c), xdev(1))
        col_copy(t, "x-1", cbuf, chunk(x, 1), 1)
        send(t + "x-f", half(cbuf, chunk(x, 1), 1, c), half(cbuf, chunk(x, 1), 1, c), xdev(3))

    def forward_second(t, rbuf, cbuf):
        recv(t + "y-o")
        send(t + "y-f", grp(rbuf, chunk(y, 1), o), grp(rbuf, chunk(y, 1), o), ydev(3))
        col_copy(t, "x+1", cbuf, chunk(x, 3), 1)
        col_copy(t, "x-0", cbuf, chunk(x, 1), 0)

    def gather_end(t, cbuf):
        col_copy(t, "x+f", cbuf, chunk(x, 2), 0)
        col_copy(t, "x-f", cbuf, chunk(x, 2), 1)
        for came in ("y+o", "y-c", "y+f", "y-f"):
            recv(t + came)
        for came in ("", "x+0", "x-1", "x+1", "x-0", "x+f", "x-f"):
            recv(t + "s" + came)

    row_own("R", RR, grp(RR, y, c), SWR)
    col_own("R", CR, CR.at[x, :, pl.ds(4 * c, 4)])
    row_sib("R", RR)
    send("Lsw", rl_in.at[pl.ds(2 * o, 2)], grp(RL, y, c), sib)
    forward_first("R", RR, CR)
    forward_second("R", RR, CR)
    send("Ly+c", rl_in.at[pl.ds(2 * c, 2)], grp(RL, y, c), ydev(1))
    send("Ly-c", rl_in.at[pl.ds(2 * c, 2)], grp(RL, y, c), ydev(3))
    col_own("L", CL, cl_in)
    row_sib("L", RL)

    for copy in local:
        copy.wait()
    h, m, l = split3(dot_nt(sk[...], TRO[...]))
    own = dot_nn(jnp.concatenate([h, m, l], axis=0), TLO[...])
    TT[...] = own[0:K] + own[K:2 * K] + own[2 * K:]

    gather_end("R", CR)

    blocks = lax.broadcasted_iota(jnp.int32, (256, 256), 0) // K == lax.broadcasted_iota(jnp.int32, (256, 256), 1) // K

    def couple(n, _):
        q, g = lax.div(n, 2), lax.rem(n, 2)
        i, j = lax.div(q, 4), lax.rem(q, 4)
        acc = jnp.zeros((256, 256), F32)
        for b in range(NX):
            acc = acc + dot_nt(
                RR[b, i, pl.ds(4 * g, 4)].reshape(256, CH), CR[b, j, pl.ds(4 * g, 4)].reshape(256, CH)
            )
        hi, lo = split2(jnp.where(blocks, -acc, 0.0))
        BDh[q, g] = hi
        BDl[q, g] = lo
        return 0

    lax.fori_loop(0, 16, couple, 0)

    forward_first("L", RL, CL)
    forward_second("L", RL, CL)
    gather_end("L", CL)

    def col_sketch(j, _):
        acc = jnp.zeros((K, 512), F32)
        for a in range(NX):
            acc = acc + dot_nt(sk[:, CH * a:CH * (a + 1)], CL[a, j].reshape(512, CH))
        hi, lo = split2(acc)
        CS[j, 0:K] = hi
        CS[j, K:2 * K] = lo
        return 0

    lax.fori_loop(0, 4, col_sketch, 0)

    def mix_tile(q, _):
        j = lax.rem(q, 4)
        for g in range(2):
            both = CS[j, :, 256 * g:256 * (g + 1)]
            p = dot_nt(both, BDh[q, g])
            mix = p[0:K] + p[K:] + dot_nt(both[0:K], BDl[q, g])
            hi, lo = split2(mix)
            MX[q, 0:K, 256 * g:256 * (g + 1)] = hi
            MX[q, K:2 * K, 256 * g:256 * (g + 1)] = lo
        return 0

    lax.fori_loop(0, 8, mix_tile, 0)

    def s_tile(q):
        i = lax.div(q, 4)
        both = MX[q]
        for b in range(NX):
            p = dot_nn(both, RL[b, i].reshape(512, CH))
            S[q, :, CH * b:CH * (b + 1)] = p[0:K] + p[K:]

    def up(s):
        return lax.rem(z + NZ - 1 - s, NZ)

    def down(s):
        return lax.rem(z + 1 + s, NZ)

    for s in range(NZ - 1):
        if s == 0:
            s_tile(up(0))
        for u in range(2):
            if s > 0:
                recv(f"S+{s - 1}{u}")
                S[up(s), 16 * u:16 * u + 16] += RSP[s - 1, u]
            send(f"S+{s}{u}", S.at[up(s), pl.ds(16 * u, 16)], RSP.at[s, u], zdev(1))
        if s == 0:
            s_tile(down(0))
        for u in range(2, 4):
            if s > 0:
                recv(f"S-{s - 1}{u}")
                S[down(s), 16 * u:16 * u + 16] += RSM[s - 1, u - 2]
            send(f"S-{s}{u}", S.at[down(s), pl.ds(16 * u, 16)], RSM.at[s, u - 2], zdev(NZ - 1))
        if s < 3:
            s_tile(up(s + 1))
        if s < 2:
            s_tile(down(s + 1))
        if s == 3:
            s_tile(z)
    for u in range(2):
        recv(f"S+{NZ - 2}{u}")
        rows = slice(16 * u, 16 * u + 16)
        SG[z, rows] = S[z, rows] + RSP[NZ - 2, u] + TT[rows]
    for u in range(2, 4):
        recv(f"S-{NZ - 2}{u}")
        rows = slice(16 * u, 16 * u + 16)
        SG[z, rows] = S[z, rows] + RSM[NZ - 2, u - 2] + TT[rows]

    def pass_on(s, way, hs):
        owner = lax.rem(z + NZ - (s - 1), NZ) if way == "+" else lax.rem(z + s - 1, NZ)
        for h in hs:
            if s > 1:
                recv(f"G{way}{s - 1}{h}")
            part = SG.at[owner, pl.ds(32 * h, 32)]
            send(f"G{way}{s}{h}", part, part, zdev(1 if way == "+" else NZ - 1))

    def tile_back(q):
        i = lax.div(q, 4)
        hi, lo = split2(SG[q])
        both = jnp.concatenate([hi, lo], axis=0)
        acc = jnp.zeros((2 * K, 512), F32)
        for b in range(NX):
            acc = acc + dot_nt(both[:, CH * b:CH * (b + 1)], RL[b, i].reshape(512, CH))
        hi, lo = split2(acc[0:K] + acc[K:])
        both = jnp.concatenate([hi, lo], axis=0)
        for g in range(2):
            cols = slice(256 * g, 256 * (g + 1))
            p = dot_nn(both[:, cols], BDh[q, g])
            BC[q, :, cols] = p[0:K] + p[K:] + dot_nn(hi[:, cols], BDl[q, g])

    lane = lax.broadcasted_iota(jnp.int32, (K, 2 * K), 1)
    sub = lax.broadcasted_iota(jnp.int32, (K, 2 * K), 0)
    lane1 = lax.broadcasted_iota(jnp.int32, (1, 2 * K), 1)
    sub1 = lax.broadcasted_iota(jnp.int32, (K, 1), 0)

    def inverse_factor(v):
        wide = jnp.concatenate([v, jnp.zeros_like(v)], axis=0)
        gram = lax.dot_general(v, wide, (((1,), (1,)), ((), ())), precision=HI, preferred_element_type=F32)
        X[...] = jnp.where(lane == sub + K, 1.0, gram)

        def step(n, _):
            full = X[...]
            row = X[pl.ds(n, 1), :]
            pivot = jnp.sum(jnp.where(lane1 == n, row, 0.0), axis=1, keepdims=True)
            col = jnp.sum(jnp.where(lane == n, full, 0.0), axis=1, keepdims=True)
            X[...] = full - jnp.where(sub1 > n, col, 0.0) * (row / pivot)
            return 0

        lax.fori_loop(0, K, step, 0)
        full = X[...]
        pivots = jnp.sum(jnp.where(lane == sub, full, 0.0), axis=1, keepdims=True)
        return full[:, K:] * (1.0 / jnp.sqrt(pivots))

    def dot_hi(a, b):
        return lax.dot_general(a, b, (((1,), (0,)), ((), ())), precision=HI, preferred_element_type=F32)

    pass_on(1, "+", (0, 1))
    pass_on(1, "-", (1, 0))
    first = inverse_factor(SG[z])
    WW[z] = first
    Q[...] = dot_hi(first, SG[z])
    pass_on(2, "+", (0, 1))
    pass_on(2, "-", (1, 0))
    tile_back(lax.rem(z + 7, NZ))
    tile_back(lax.rem(z + 1, NZ))
    second = inverse_factor(Q[...])
    WW[z] = dot_hi(second, WW[z])
    for k in range(1, NZ):
        send(f"W{k}", WW.at[z], WW.at[z], zdev(k))
    pass_on(3, "+", (0, 1))
    pass_on(3, "-", (1, 0))
    tile_back(lax.rem(z + 6, NZ))
    tile_back(lax.rem(z + 2, NZ))
    tile_back(z)
    pass_on(4, "+", (0,))
    pass_on(4, "-", (1,))
    h, m, l = split3(dot_hi(WW[z], SG[z]))
    own = dot_nt(jnp.concatenate([h, m, l], axis=0), TLO[...])
    h, m, l = split3(own[0:K] + own[K:2 * K] + own[2 * K:])
    own = dot_nn(jnp.concatenate([h, m, l], axis=0), TRO[...])
    TT[...] = own[0:K] + own[K:2 * K] + own[2 * K:]
    recv("G+31")
    tile_back(lax.rem(z + 5, NZ))
    recv("G-30")
    tile_back(lax.rem(z + 3, NZ))
    recv("G+40")
    recv("G-41")
    tile_back(lax.rem(z + 4, NZ))
    for k in range(1, NZ):
        recv(f"W{k}")

    def right_tile(q, _):
        j = lax.rem(q, 4)
        hi, lo = split2(dot_hi(WW[q], BC[q]))
        both = jnp.concatenate([hi, lo], axis=0)
        mine = jnp.where(q == z, 1.0, 0.0)
        for a in range(NX):
            cols = slice(CH * a, CH * (a + 1))
            p = dot_nn(both, CL[a, j].reshape(512, CH))
            RT[q, :, cols] = p[0:K] + p[K:] + mine * TT[:, cols]
        return 0

    def rows_of(chip):
        return pl.ds(pl.multiple_of(8 * chip, 8), 8)

    keep0 = c == 0
    scale = math.sqrt(NB)

    def basis_rows(q):
        v = scale * dot_hi(WW[q, rows_of(z), :], SG[q])
        FSL[4 * q:4 * q + 4] = jnp.where(keep0, v[4:8], v[0:4])
        outl[2 * c + q // 4, q % 4] = jnp.where(keep0, v[0:4], v[4:8])

    lax.fori_loop(0, 4, right_tile, 0)
    for s in range(NZ - 1):
        for u in range(2):
            tiles = slice(2 * u, 2 * u + 2)
            if s > 0:
                recv(f"P+{s - 1}{u}")
                RT[tiles, rows_of(up(s))] += RQP[s - 1, u]
            send(f"P+{s}{u}", RT.at[pl.ds(2 * u, 2), rows_of(up(s))], RQP.at[s, u], zdev(1))
        if s == 0:
            lax.fori_loop(4, 8, right_tile, 0)
        for u in range(2, 4):
            tiles = slice(2 * u, 2 * u + 2)
            if s > 0:
                recv(f"P-{s - 1}{u}")
                RT[tiles, rows_of(down(s))] += RQM[s - 1, u - 2]
            send(f"P-{s}{u}", RT.at[pl.ds(2 * u, 2), rows_of(down(s))], RQM.at[s, u - 2], zdev(NZ - 1))
        if s == 0:
            basis_rows(7)
        basis_rows(s)
    send("FL", FSL, FRL, sib)

    for u in range(4):
        way, buf = ("+", RQP) if u < 2 else ("-", RQM)
        recv(f"P{way}{NZ - 2}{u}")
        for q in (2 * u, 2 * u + 1):
            v = (1.0 / scale) * (RT[q, rows_of(z)] + buf[NZ - 2, u % 2, q % 2])
            FSR[4 * q:4 * q + 4] = jnp.where(keep0, v[4:8], v[0:4])
            outr[2 * c + q // 4, q % 4] = jnp.where(keep0, v[0:4], v[4:8])
    send("FR", FSR, FRR, sib)
    recv("FL")
    for q in range(8):
        outl[2 * o + q // 4, q % 4] = FRL[4 * q:4 * q + 4]
    recv("FR")
    for q in range(8):
        outr[2 * o + q // 4, q % 4] = FRR[4 * q:4 * q + 4]
    for copy in descs.values():
        copy.wait_send()


N_COPIES = 2 * (7 + 6 + 7) + 28 + 14 + 7 + 28 + 2


def on_device(
    tile_left, tile_right, row_left, row_right, col_left, col_right, row_mask, col_mask, sketch
):
    vmem = pl.BlockSpec(memory_space=pltpu.VMEM)
    smem = pl.BlockSpec(memory_space=pltpu.SMEM)
    hbm = pl.BlockSpec(memory_space=pl.ANY)
    out = jax.ShapeDtypeStruct((4, 4, 4, NB), F32)
    return pl.pallas_call(
        kernel,
        out_shape=(out, out),
        in_specs=[smem, smem, hbm, hbm, hbm, vmem, hbm, vmem, vmem],
        out_specs=(vmem, vmem),
        scratch_shapes=[
            pltpu.VMEM((NX, 2, 8, K, CH), BF16),
            pltpu.VMEM((NX, 2, 8, K, CH), BF16),
            pltpu.VMEM((NX, 4, 8, K, CH), BF16),
            pltpu.VMEM((NX, 4, 8, K, CH), BF16),
            pltpu.VMEM((2, 4, K, CH), BF16),
            pltpu.VMEM((8, 2, 256, 256), BF16),
            pltpu.VMEM((8, 2, 256, 256), BF16),
            pltpu.VMEM((4, 2 * K, 512), BF16),
            pltpu.VMEM((8, 2 * K, 512), BF16),
            pltpu.VMEM((8, K, NB), F32),
            pltpu.VMEM((8, K, NB), F32),
            pltpu.VMEM((8, K, NB), F32),
            pltpu.VMEM((NZ - 1, 2, 16, NB), F32),
            pltpu.VMEM((NZ - 1, 2, 16, NB), F32),
            pltpu.VMEM((NZ - 1, 2, 2, 8, NB), F32),
            pltpu.VMEM((NZ - 1, 2, 2, 8, NB), F32),
            pltpu.VMEM((K, NB), F32),
            pltpu.VMEM((K, NB), BF16),
            pltpu.VMEM((K, NB), BF16),
            pltpu.VMEM((K, 2 * K), F32),
            pltpu.VMEM((K, NB), F32),
            pltpu.VMEM((8, K, K), F32),
            pltpu.VMEM((8, K, 512), F32),
            pltpu.VMEM((32, NB), F32),
            pltpu.VMEM((32, NB), F32),
            pltpu.VMEM((32, NB), F32),
            pltpu.VMEM((32, NB), F32),
            pltpu.SemaphoreType.DMA((N_COPIES,)),
            pltpu.SemaphoreType.DMA((N_COPIES,)),
            pltpu.SemaphoreType.DMA((4,)),
        ],
        compiler_params=pltpu.CompilerParams(
            collective_id=0, has_side_effects=True, vmem_limit_bytes=56 * 1024 * 1024
        ),
        name="trailing_update",
    )(row_mask, col_mask, tile_left, tile_right, row_left, row_right, col_left, col_right, sketch)


def solution(mesh):
    in_specs = (
        P("row", "col", None, None),
        P("row", "col", None, None),
        P("row", "depth", None, "col"),
        P("row", "depth", None, "col"),
        P("col", "depth", None, "row"),
        P("col", "depth", None, "row"),
        P("row", "depth"),
        P("col", "depth"),
        P(),
    )
    out_specs = (P("row", "col", "depth", None), P("row", "col", "depth", None))
    return jax.shard_map(
        on_device, mesh=mesh, in_specs=in_specs, out_specs=out_specs, check_vma=False
    )
```

time: 818 us -> 152 us (0.19)
  waiting for transfers between devices: 383 us -> 0 us
  other arithmetic: 351 us -> 0 us
  Pallas kernels: 0 us -> 148 us
  matrix products: 58.2 us -> 0 us
  between operations: 15.1 us -> 0.64 us
    another operation x12 -> x0, other arithmetic: 347 us -> none  [the longest x7 189 us: orthonormalize(): factor = jnp.linalg.cholesky(gram_mat)]
    pallas_call x0 -> x1, Pallas kernels: none -> 148 us  [on_device(): pl.pallas_call(kernel, out_shape=(out, out), in_specs=[smem, smem, hbm, h...]
    all_gather x4 -> x0, waiting for transfers between devices: 147 us -> none  [the longest x1 39.9 us: on_device(): lax.all_gather(row_right, 'col', axis=3, tiled=True)]
    psum x1 -> x0, waiting for transfers between devices: 120 us -> none  [on_device(): summed = lax.psum(partial_sketch, 'depth')]
    unnamed x7 -> x0, waiting for transfers between devices: 116 us -> none
    dot_general x13 -> x0, matrix products: 46.8 us -> none  [the longest x2 8.04 us: orthonormalize(): jnp.einsum('ijtn,ijsn->ijts', sketched, sketched, precision=exact_mode)]
    another operation x2 -> x0, matrix products: 11.4 us -> none  [orthonormalize(): sketched = jax.scipy.linalg.solve_triangular(factor, sketched, lower=True)]
  transfers between devices with their start and end apart: 6 -> 0, of which waited for: 6 -> 0; matrix products, arithmetic and copies ran while one was open for 2% -> 0% of each run, Pallas kernels for 0% -> 0%
where the time goes in v1:
time: 152 us
  Pallas kernels  148 us (97%)
  local copies, waits for them, and re-layouts  3.34 us (2%)
    pallas_call x1, Pallas kernels, on_device(): pl.pallas_call(kernel, out_shape=(out, out), in_specs=[smem, smem, hbm, h...  148 us
    unnamed x2, local copies, waits for them, and re-layouts  3.34 us

profile of v1, /device:TPU:1, one launch (start us, length us, event | category | flops | bytes accessed | tf_op | source)
XLA Modules:
  0.0 152.1 jit_solution(933100949703576783)
XLA Ops:
  0.6 148.1 %trailing_update.1 = (f32[4,4,4,1024]{3,2,1,0:T(4,128)}, f32[4,4,4,1024]{3,2,1,0:T(4,128)}) custom-call(s32[4,4]{1,0:T(4,128)} %rm.1, s32[4,4]{1,0:T(4,128)} %cm.1, bf16[4,4,64,1024]{3,2,1,0:T(8,128)(2,1)} %tl_in.1, bf16[4,4,64,1024]{3,2,1,0:T(8,128)(2,1)} %tr_in.1, bf16[4,4,64,256]{3,2,1,0:T(8,128)(2,1)} %rl_in.1, bf16[4,4,64,256]{3,2,1,0:T(8,128)(2,1)} %rr_in.1, ...), custom_call_target="tpu_custom_call" | custom-call | tf_op jit(solution)/shard_map/trailing_update/pallas_call | solution.py:429
  148.8 1.7 %copy.13 = f32[4,4,4,1024]{3,2,1,0:T(4,128)} copy(f32[4,4,4,1024]{3,2,1,0:T(4,128)} %get-tuple-element.4) | data formatting | bytes 524288
  150.5 1.7 %copy.14 = f32[4,4,4,1024]{3,2,1,0:T(4,128)} copy(f32[4,4,4,1024]{3,2,1,0:T(4,128)} %get-tuple-element.5) | data formatting | bytes 524288

commit v2 on v1

v2 whole, which is shorter than its diff:
```python
import math

import jax
import jax.numpy as jnp
from jax import lax
from jax.experimental import pallas as pl
from jax.experimental.pallas import tpu as pltpu
from jax.sharding import PartitionSpec as P

NB = 1024
K = 64
MESH = pl.DeviceIdType.MESH
F32 = jnp.float32
BF16 = jnp.bfloat16
HI = lax.Precision.HIGHEST
NZ = 8
NX = 4
CH = NB // NX


def dot_nn(a, b):
    return lax.dot_general(a, b, (((1,), (0,)), ((), ())), preferred_element_type=F32)


def dot_nt(a, b):
    return lax.dot_general(a, b, (((1,), (1,)), ((), ())), preferred_element_type=F32)


def split2(v):
    hi = v.astype(BF16)
    lo = (v - hi.astype(F32)).astype(BF16)
    return hi, lo


def split3(v):
    hi = v.astype(BF16)
    rest = v - hi.astype(F32)
    mid = rest.astype(BF16)
    lo = (rest - mid.astype(F32)).astype(BF16)
    return hi, mid, lo


def kernel(
    rm, cm, tl_in, tr_in, rl_in, rr_in, cl_in, cr_in, sk,
    outl, outr,
    RR, RL, CR, CL, WV, WS, CSP, BDh, BDl, CS, MX, S, SG, RT, RSP, RSM, RQP, RQM,
    TT, TLO, TRO, X, Q, WP, WW, BC, FSL, FSR, FRL, FRR,
    ssem, rsem, lsem,
):
    d = lax.axis_index("depth")
    x = lax.axis_index("row")
    y = lax.axis_index("col")
    c = lax.rem(d, 2)
    o = 1 - c
    z = lax.div(d, 2)

    def zdev(k):
        return (lax.rem(z + k, NZ) * 2 + c, x, y)

    def xdev(k):
        return (d, lax.rem(x + k, NX), y)

    def ydev(k):
        return (d, x, lax.rem(y + k, NX))

    sib = (z * 2 + o, x, y)

    def chunk(base, k):
        return lax.rem(base + k, NX)

    names = {}
    descs = {}

    def send(name, src, dst, dev):
        n = names.setdefault(name, len(names))
        copy = pltpu.make_async_remote_copy(
            src_ref=src, dst_ref=dst, send_sem=ssem.at[n], recv_sem=rsem.at[n],
            device_id=dev, device_id_type=MESH,
        )
        copy.start()
        descs[name] = copy

    def recv(name):
        descs[name].wait_recv()

    barrier = pltpu.get_barrier_semaphore()
    partners = [zdev(k) for k in range(1, NZ)] + [xdev(1), xdev(3), ydev(1), ydev(3), sib]
    for dev in partners:
        pl.semaphore_signal(barrier, inc=1, device_id=dev, device_id_type=MESH)
    tile_i = 2 * c + lax.div(z, 4)
    tile_j = lax.rem(z, 4)
    local = [
        pltpu.make_async_copy(rr_in.at[pl.ds(2 * c, 2)], RR.at[y, :, pl.ds(4 * c, 4)], lsem.at[0]),
        pltpu.make_async_copy(cr_in, CR.at[x, :, pl.ds(4 * c, 4)], lsem.at[1]),
        pltpu.make_async_copy(rl_in.at[pl.ds(2 * c, 2)], RL.at[y, :, pl.ds(4 * c, 4)], lsem.at[2]),
        pltpu.make_async_copy(cl_in, CL.at[x, :, pl.ds(4 * c, 4)], lsem.at[3]),
        pltpu.make_async_copy(tl_in.at[tile_i, tile_j], TLO, lsem.at[4]),
        pltpu.make_async_copy(tr_in.at[tile_i, tile_j], TRO, lsem.at[5]),
    ]
    for copy in local:
        copy.start()
    pl.semaphore_wait(barrier, len(partners))

    def grp(buf, b, g):
        return buf.at[b, :, pl.ds(4 * g, 4)]

    def half(buf, a, h):
        return buf.at[a, pl.ds(2 * h, 2), pl.ds(4 * c, 4)]

    def part(buf, a, h):
        return buf.at[a, pl.ds(2 * h, 2)]

    def block(buf, b, i, g):
        return buf.at[b, i, pl.ds(4 * (c if g == "c" else o), 4)]

    def rows_own(t, buf, src):
        for i in (0, 1):
            send(f"{t}+{i}c", src.at[2 * c + i], block(buf, y, i, "c"), ydev(1))
            send(f"{t}-{1 - i}c", src.at[2 * c + 1 - i], block(buf, y, 1 - i, "c"), ydev(3))

    def rows_other(t, buf):
        recv(t + "sw")
        for i in (0, 1):
            send(f"{t}+{i}o", block(buf, y, i, "o"), block(buf, y, i, "o"), ydev(1))
            send(f"{t}-{1 - i}o", block(buf, y, 1 - i, "o"), block(buf, y, 1 - i, "o"), ydev(3))

    def rows_on(t, buf, g):
        recv(f"{t}+0{g}")
        send(f"{t}+f{g}", block(buf, chunk(y, 3), 0, g), block(buf, chunk(y, 3), 0, g), ydev(1))
        recv(f"{t}-1{g}")
        send(f"{t}-f{g}", block(buf, chunk(y, 1), 1, g), block(buf, chunk(y, 1), 1, g), ydev(3))

    def rows_end(t):
        for came in ("+1c", "-0c", "+1o", "-0o", "+fc", "-fc", "+fo", "-fo"):
            recv(t + came)

    def cols_own(t, buf, of, src0, src1):
        send(t + "x+0", src0, of(buf, x, 0), xdev(1))
        send(t + "x-1", src1, of(buf, x, 1), xdev(3))
        send(t + "x+1", src1, of(buf, x, 1), xdev(1))
        send(t + "x-0", src0, of(buf, x, 0), xdev(3))

    def cols_on(t, buf, of):
        recv(t + "x+0")
        send(t + "x+f", of(buf, chunk(x, 3), 0), of(buf, chunk(x, 3), 0), xdev(1))
        recv(t + "x-1")
        send(t + "x-f", of(buf, chunk(x, 1), 1), of(buf, chunk(x, 1), 1), xdev(3))

    def cols_to_sib(t, buf, which):
        for came, k, h in which:
            if came in ("x+f", "x-f", "x+1", "x-0"):
                recv(t + came)
            send(t + "s" + came, half(buf, chunk(x, k), h), half(buf, chunk(x, k), h), sib)

    early = (("x+0", 3, 0), ("x-1", 1, 1))
    late = (("x+f", 2, 0), ("x-f", 2, 1), ("x+1", 3, 1), ("x-0", 1, 0))

    def cols_end(t):
        for came in ("", "x+0", "x-1", "x+1", "x-0", "x+f", "x-f"):
            recv(t + "s" + came)

    send("Rsw", rr_in.at[pl.ds(2 * o, 2)], grp(RR, y, c), sib)
    rows_own("R", RR, rr_in)
    cols_own("R", CR, half, cr_in.at[pl.ds(0, 2)], cr_in.at[pl.ds(2, 2)])
    send("Rs", cr_in, CR.at[x, :, pl.ds(4 * c, 4)], sib)
    rows_other("R", RR)
    send("Lsw", rl_in.at[pl.ds(2 * o, 2)], grp(RL, y, c), sib)
    rows_own("L", RL, rl_in)

    of_lane = lax.broadcasted_iota(jnp.int32, (1, 256), 1) // K
    for q in range(8):
        for base, buf in ((2 * c, WV.at[c]), (2 * o, WS)):
            row = jnp.zeros((1, 256), F32)
            for kk in range(4):
                weight = (rm[base + q // 4, kk] * cm[q % 4, kk]).astype(F32)
                row = row + jnp.where(of_lane == kk, weight, 0.0)
            buf[q:q + 1, :] = row
    send("M", WS, WV.at[c], sib)
    for copy in local:
        copy.wait()

    def part_sketch(j, _):
        CSP[x, j] = dot_nt(
            sk[:, pl.ds(pl.multiple_of(CH * x, CH), CH)], CL[x, j, pl.ds(4 * c, 4)].reshape(256, CH)
        )
        return 0

    lax.fori_loop(0, 4, part_sketch, 0)
    cols_own("C", CSP, part, part(CSP, x, 0), part(CSP, x, 1))
    rows_on("R", RR, "c")
    cols_on("R", CR, half)
    rows_on("R", RR, "o")
    rows_other("L", RL)
    cols_to_sib("R", CR, early)

    h, m, l = split3(dot_nt(sk[...], TRO[...]))
    own = dot_nn(jnp.concatenate([h, m, l], axis=0), TLO[...])
    TT[...] = own[0:K] + own[K:2 * K] + own[2 * K:]

    rows_on("L", RL, "c")
    rows_end("R")
    cols_to_sib("R", CR, late)
    cols_on("C", CSP, part)
    cols_end("R")
    recv("M")

    blocks = lax.broadcasted_iota(jnp.int32, (256, 256), 0) // K == lax.broadcasted_iota(jnp.int32, (256, 256), 1) // K

    def couple(n, _):
        q, g = lax.div(n, 2), lax.rem(n, 2)
        i, j = lax.div(q, 4), lax.rem(q, 4)
        acc = jnp.zeros((256, 256), F32)
        for b in range(NX):
            acc = acc + dot_nt(
                RR[b, i, pl.ds(4 * g, 4)].reshape(256, CH), CR[b, j, pl.ds(4 * g, 4)].reshape(256, CH)
            )
        hi, lo = split2(jnp.where(blocks, -acc * WV[g, pl.ds(q, 1), :], 0.0))
        BDh[q, g] = hi
        BDl[q, g] = lo
        return 0

    lax.fori_loop(0, 8, couple, 0)
    rows_on("L", RL, "o")
    lax.fori_loop(8, 16, couple, 0)
    for came in ("x+f", "x-f", "x+1", "x-0"):
        recv("C" + came)

    def col_sketch(j, _):
        hi, lo = split2((CSP[0, j] + CSP[1, j]) + (CSP[2, j] + CSP[3, j]))
        CS[j, c, 0:K] = hi
        CS[j, c, K:2 * K] = lo
        return 0

    lax.fori_loop(0, 4, col_sketch, 0)
    send("CS", CS.at[:, c], CS.at[:, c], sib)
    cols_own("L", CL, half, half(CL, x, 0), half(CL, x, 1))
    send("Ls", CL.at[x, :, pl.ds(4 * c, 4)], CL.at[x, :, pl.ds(4 * c, 4)], sib)
    recv("CS")

    def mix_tile(q, _):
        j = lax.rem(q, 4)
        for g in range(2):
            both = CS[j, g]
            p = dot_nt(both, BDh[q, g])
            mix = p[0:K] + p[K:] + dot_nt(both[0:K], BDl[q, g])
            hi, lo = split2(mix)
            MX[q, 0:K, 256 * g:256 * (g + 1)] = hi
            MX[q, K:2 * K, 256 * g:256 * (g + 1)] = lo
        return 0

    lax.fori_loop(0, 8, mix_tile, 0)
    rows_end("L")

    def s_tile(q):
        i = lax.div(q, 4)
        both = MX[q]
        for b in range(NX):
            p = dot_nn(both, RL[b, i].reshape(512, CH))
            S[q, :, CH * b:CH * (b + 1)] = p[0:K] + p[K:]

    def at(k):
        return lax.rem(z + k, NZ)

    def sum_send(way, s, u):
        buf, dev, tile = (RSP, zdev(1), at(4 - s)) if way == "+" else (RSM, zdev(7), at(4 + s))
        rows = slice(16 * u, 16 * u + 16)
        if s > 1 or (s == 1 and (u < 2) == (way == "+")):
            recv(f"S{way}{s - 1}{u}")
            S[tile, rows] += buf[s - 1, u]
        send(f"S{way}{s}{u}", S.at[tile, pl.ds(16 * u, 16)], buf.at[s, u], dev)

    s_tile(at(4))
    for u in (0, 2, 1, 3):
        sum_send("+" if u < 2 else "-", 0, u)
    s_tile(at(3))
    for u in (2, 3):
        sum_send("+", 1, u)
    s_tile(at(5))
    for u in (0, 1):
        sum_send("-", 1, u)
    s_tile(at(2))
    s_tile(at(6))
    for u in (0, 1):
        sum_send("+", 1, u)
        sum_send("-", 1, u + 2)
    s_tile(at(1))
    s_tile(at(7))
    cols_on("L", CL, half)
    for u in (2, 3, 0, 1):
        sum_send("+", 2, u)
        sum_send("-", 2, (u + 2) % 4)
    s_tile(z)
    cols_to_sib("L", CL, early)
    for u in (2, 3, 0, 1):
        sum_send("+", 3, u)
        sum_send("-", 3, (u + 2) % 4)
    cols_to_sib("L", CL, late)

    def pass_on(s, u, way):
        if s == 4 and (u < 2) != (way == "+"):
            return
        if s > 1:
            recv(f"G{way}{s - 1}{u}")
        part_of = SG.at[at(9 - s) if way == "+" else at(s - 1), pl.ds(16 * u, 16)]
        send(f"G{way}{s}{u}", part_of, part_of, zdev(1 if way == "+" else 7))

    def pass_both(s, n):
        pass_on(s, n, "+")
        pass_on(s, (n + 2) % 4, "-")

    for u in (0, 2, 1, 3):
        recv(f"S+3{u}")
        recv(f"S-3{u}")
        rows = slice(16 * u, 16 * u + 16)
        SG[z, rows] = (S[z, rows] + TT[rows]) + (RSP[3, u] + RSM[3, u])
    for u in range(4):
        pass_both(1, u)

    def tile_back(q):
        i = lax.div(q, 4)
        hi, lo = split2(SG[q])
        both = jnp.concatenate([hi, lo], axis=0)
        acc = jnp.zeros((2 * K, 512), F32)
        for b in range(NX):
            acc = acc + dot_nt(both[:, CH * b:CH * (b + 1)], RL[b, i].reshape(512, CH))
        hi, lo = split2(acc[0:K] + acc[K:])
        both = jnp.concatenate([hi, lo], axis=0)
        for g in range(2):
            cols = slice(256 * g, 256 * (g + 1))
            p = dot_nn(both[:, cols], BDh[q, g])
            BC[q, :, cols] = p[0:K] + p[K:] + dot_nn(hi[:, cols], BDl[q, g])

    lane = lax.broadcasted_iota(jnp.int32, (K, 2 * K), 1)
    sub = lax.broadcasted_iota(jnp.int32, (K, 2 * K), 0)
    lane1 = lax.broadcasted_iota(jnp.int32, (1, 2 * K), 1)
    sub1 = lax.broadcasted_iota(jnp.int32, (K, 1), 0)

    def inverse_factor(v, between=None):
        wide = jnp.concatenate([v, jnp.zeros_like(v)], axis=0)
        gram = lax.dot_general(v, wide, (((1,), (1,)), ((), ())), precision=HI, preferred_element_type=F32)
        X[...] = jnp.where(lane == sub + K, 1.0, gram)

        def step(t, _):
            n = 4 * t
            full = X[...]
            rows = [X[pl.ds(n + e, 1), :] for e in range(4)]
            top = {
                (e, f): jnp.sum(jnp.where(lane1 == n + f, rows[e], 0.0), axis=1, keepdims=True)
                for e in range(4) for f in range(e, 4)
            }
            cols = [jnp.sum(jnp.where(lane == n + e, full, 0.0), axis=1, keepdims=True) for e in range(4)]
            for e in range(4):
                inv = 1.0 / top[e, e]
                for f in range(e + 1, 4):
                    ratio = top[e, f] * inv
                    rows[f] = rows[f] - ratio * rows[e]
                    cols[f] = cols[f] - ratio * cols[e]
                    for w in range(f, 4):
                        top[f, w] = top[f, w] - ratio * top[e, w]
                full = full - jnp.where(sub1 > n + e, cols[e], 0.0) * (rows[e] * inv)
            X[...] = full
            return 0

        lax.fori_loop(0, K // 8, step, 0)
        if between:
            between()
        lax.fori_loop(K // 8, K // 4, step, 0)
        full = X[...]
        pivots = jnp.sum(jnp.where(lane == sub, full, 0.0), axis=1, keepdims=True)
        return full[:, K:] * (1.0 / jnp.sqrt(pivots))

    def dot_hi(a, b):
        return lax.dot_general(a, b, (((1,), (0,)), ((), ())), precision=HI, preferred_element_type=F32)

    first = inverse_factor(SG[z])
    Q[...] = dot_hi(first, SG[z])
    pass_both(2, 0)
    second = inverse_factor(Q[...], lambda: pass_both(2, 1))
    whole = dot_hi(second, first)
    WP[z, :, 0:K] = whole[32:64]
    WP[z, :, K:2 * K] = whole[0:32]
    pass_both(2, 2)
    for k in range(1, NZ):
        send(f"W{k}", WP.at[z], WP.at[z], zdev(k))
    tile_back(z)
    pass_both(2, 3)
    pass_both(3, 0)
    tile_back(at(1))
    pass_both(3, 1)
    tile_back(at(7))
    pass_both(3, 2)
    pass_both(4, 0)
    h, m, l = split3(dot_hi(whole, SG[z]))
    own = dot_nt(jnp.concatenate([h, m, l], axis=0), TLO[...])
    h, m, l = split3(own[0:K] + own[K:2 * K] + own[2 * K:])
    own = dot_nn(jnp.concatenate([h, m, l], axis=0), TRO[...])
    TT[...] = own[0:K] + own[K:2 * K] + own[2 * K:]
    pass_both(3, 3)
    pass_both(4, 1)
    tile_back(at(2))
    tile_back(at(6))
    for u in (2, 3):
        recv(f"G+3{u}")
    tile_back(at(5))
    for u in (0, 1):
        recv(f"G-3{u}")
    tile_back(at(3))
    for u in range(4):
        recv(f"G{'+' if u < 2 else '-'}4{u}")
    tile_back(at(4))
    for k in range(1, NZ):
        recv(f"W{k}")
    cols_end("L")

    def unpack(q, _):
        WW[q, 32:64] = WP[q, :, 0:K]
        WW[q, 0:32] = WP[q, :, K:2 * K]
        return 0

    lax.fori_loop(0, 8, unpack, 0)

    def right_tile(q, _):
        j = lax.rem(q, 4)
        hi, lo = split2(dot_hi(WW[q], BC[q]))
        both = jnp.concatenate([hi, lo], axis=0)
        mine = jnp.where(q == z, 1.0, 0.0)
        for a in range(NX):
            cols = slice(CH * a, CH * (a + 1))
            p = dot_nn(both, CL[a, j].reshape(512, CH))
            RT[q, :, cols] = p[0:K] + p[K:] + mine * TT[:, cols]
        return 0

    def rows_of(chip):
        return pl.ds(pl.multiple_of(8 * chip, 8), 8)

    keep0 = c == 0

    def basis_rows(q):
        v = dot_hi(WW[q, rows_of(z), :], SG[q])
        FSL[4 * q:4 * q + 4] = jnp.where(keep0, v[4:8], v[0:4])
        outl[2 * c + q // 4, q % 4] = jnp.where(keep0, v[0:4], v[4:8])

    def pair(buf, u, chip):
        return buf.at[pl.ds(2 * u, 2), rows_of(chip)]

    for u in range(4):
        lax.fori_loop(2 * u, 2 * u + 2, right_tile, 0)
        if u < 2:
            send(f"P+0{u}", pair(RT, u, at(4)), RQP.at[0, u], zdev(1))
            send(f"P-1{u}", pair(RT, u, at(5)), RQM.at[1, u], zdev(7))
        else:
            send(f"P-0{u}", pair(RT, u, at(4)), RQM.at[0, u], zdev(7))
            send(f"P+1{u}", pair(RT, u, at(3)), RQP.at[1, u], zdev(1))
    basis_rows(0)
    basis_rows(1)
    for s in range(1, 4):
        for u in range(4):
            for way, buf, dev, chip in (("+", RQP, zdev(1), at(4 - s)), ("-", RQM, zdev(7), at(4 + s))):
                if s == 1 and (u < 2) != (way == "+"):
                    continue
                recv(f"P{way}{s - 1}{u}")
                RT[2 * u:2 * u + 2, rows_of(chip)] += buf[s - 1, u]
                send(f"P{way}{s}{u}", pair(RT, u, chip), buf.at[s, u], dev)
        basis_rows(2 * s)
        basis_rows(2 * s + 1)
    send("FL", FSL, FRL, sib)

    for u in range(4):
        recv(f"P+3{u}")
        recv(f"P-3{u}")
        for q in (2 * u, 2 * u + 1):
            v = RT[q, rows_of(z)] + (RQP[3, u, q % 2] + RQM[3, u, q % 2])
            FSR[4 * q:4 * q + 4] = jnp.where(keep0, v[4:8], v[0:4])
            outr[2 * c + q // 4, q % 4] = jnp.where(keep0, v[0:4], v[4:8])
    send("FR", FSR, FRR, sib)
    recv("FL")
    for q in range(8):
        outl[2 * o + q // 4, q % 4] = FRL[4 * q:4 * q + 4]
    recv("FR")
    for q in range(8):
        outr[2 * o + q // 4, q % 4] = FRR[4 * q:4 * q + 4]
    for copy in descs.values():
        copy.wait_send()


N_COPIES = 2 * (13 + 6 + 7) + 6 + 2 + 28 + 28 + 7 + 28 + 2


def on_device(
    tile_left, tile_right, row_left, row_right, col_left, col_right, row_mask, col_mask, sketch
):
    vmem = pl.BlockSpec(memory_space=pltpu.VMEM)
    smem = pl.BlockSpec(memory_space=pltpu.SMEM)
    hbm = pl.BlockSpec(memory_space=pl.ANY)
    out = jax.ShapeDtypeStruct((4, 4, 4, NB), F32)
    basis, projection = pl.pallas_call(
        kernel,
        out_shape=(out, out),
        in_specs=[smem, smem, hbm, hbm, hbm, hbm, hbm, hbm, vmem],
        out_specs=(vmem, vmem),
        scratch_shapes=[
            pltpu.VMEM((NX, 2, 8, K, CH), BF16),
            pltpu.VMEM((NX, 2, 8, K, CH), BF16),
            pltpu.VMEM((NX, 4, 8, K, CH), BF16),
            pltpu.VMEM((NX, 4, 8, K, CH), BF16),
            pltpu.VMEM((2, 8, 256), F32),
            pltpu.VMEM((8, 256), F32),
            pltpu.VMEM((NX, 4, K, 256), F32),
            pltpu.VMEM((8, 2, 256, 256), BF16),
            pltpu.VMEM((8, 2, 256, 256), BF16),
            pltpu.VMEM((4, 2, 2 * K, 256), BF16),
            pltpu.VMEM((8, 2 * K, 512), BF16),
            pltpu.VMEM((8, K, NB), F32),
            pltpu.VMEM((8, K, NB), F32),
            pltpu.VMEM((8, K, NB), F32),
            pltpu.VMEM((4, 4, 16, NB), F32),
            pltpu.VMEM((4, 4, 16, NB), F32),
            pltpu.VMEM((4, 4, 2, 8, NB), F32),
            pltpu.VMEM((4, 4, 2, 8, NB), F32),
            pltpu.VMEM((K, NB), F32),
            pltpu.VMEM((K, NB), BF16),
            pltpu.VMEM((K, NB), BF16),
            pltpu.VMEM((K, 2 * K), F32),
            pltpu.VMEM((K, NB), F32),
            pltpu.VMEM((8, 32, 2 * K), F32),
            pltpu.VMEM((8, K, K), F32),
            pltpu.VMEM((8, K, 512), F32),
            pltpu.VMEM((32, NB), F32),
            pltpu.VMEM((32, NB), F32),
            pltpu.VMEM((32, NB), F32),
            pltpu.VMEM((32, NB), F32),
            pltpu.SemaphoreType.DMA((N_COPIES,)),
            pltpu.SemaphoreType.DMA((N_COPIES,)),
            pltpu.SemaphoreType.DMA((6,)),
        ],
        compiler_params=pltpu.CompilerParams(
            collective_id=0, has_side_effects=True, vmem_limit_bytes=56 * 1024 * 1024
        ),
        name="trailing_update",
    )(row_mask, col_mask, tile_left, tile_right, row_left, row_right, col_left, col_right, sketch)
    return basis * math.sqrt(NB), projection * (1.0 / math.sqrt(NB))


def solution(mesh):
    in_specs = (
        P("row", "col", None, None),
        P("row", "col", None, None),
        P("row", "depth", None, "col"),
        P("row", "depth", None, "col"),
        P("col", "depth", None, "row"),
        P("col", "depth", None, "row"),
        P("row", "depth"),
        P("col", "depth"),
        P(),
    )
    out_specs = (P("row", "col", "depth", None), P("row", "col", "depth", None))
    return jax.shard_map(
        on_device, mesh=mesh, in_specs=in_specs, out_specs=out_specs, check_vma=False
    )
```

time: 152 us -> 124 us (0.82)
  Pallas kernels: 148 us -> 122 us
  local copies, waits for them, and re-layouts: 3.34 us -> 0 us
  other arithmetic: 0 us -> 1.99 us
    pallas_call x1, Pallas kernels: 148 us -> 122 us  [on_device(): pl.pallas_call(kernel, out_shape=(out, out), in_specs=[smem, smem, hbm, h...]
    unnamed x2 -> x0, local copies, waits for them, and re-layouts: 3.34 us -> none
    mul x0 -> x1, other arithmetic: none -> 1.99 us  [on_device(): return (basis * math.sqrt(NB), projection * (1.0 / math.sqrt(NB)))]
where the time goes in v2:
time: 124 us
  Pallas kernels  122 us (98%)
  other arithmetic  1.99 us (2%)
    pallas_call x1, Pallas kernels, on_device(): pl.pallas_call(kernel, out_shape=(out, out), in_specs=[smem, smem, hbm, h...  122 us

profile of v2, /device:TPU:1, one launch (start us, length us, event | category | flops | bytes accessed | tf_op | source)
XLA Modules:
  0.0 124.2 jit_solution(11742631846171572714)
XLA Ops:
  0.6 121.6 %trailing_update.1 = (f32[4,4,4,1024]{3,2,1,0:T(4,128)}, f32[4,4,4,1024]{3,2,1,0:T(4,128)}) custom-call(s32[4,4]{1,0:T(4,128)} %rm.1, s32[4,4]{1,0:T(4,128)} %cm.1, bf16[4,4,64,1024]{3,2,1,0:T(8,128)(2,1)} %tl_in.1, bf16[4,4,64,1024]{3,2,1,0:T(8,128)(2,1)} %tr_in.1, bf16[4,4,64,256]{3,2,1,0:T(8,128)(2,1)} %rl_in.1, bf16[4,4,64,256]{3,2,1,0:T(8,128)(2,1)} %rr_in.1, ...), custom_call_target="tpu_custom_call" | custom-call | tf_op jit(solution)/shard_map/trailing_update/pallas_call | solution.py:496
  122.2 2.0 %broadcast_multiply_fusion = (f32[4,4,4,1024]{3,2,1,0:T(4,128)}, f32[4,4,4,1024]{3,2,1,0:T(4,128)}) fusion(f32[4,4,4,1024]{3,2,1,0:T(4,128)} %get-tuple-element.5, f32[4,4,4,1024]{3,2,1,0:T(4,128)} %get-tuple-element.4), kind=kLoop, calls=%fused_computation | loop fusion | flops 131072 | bytes 1048576 | tf_op jit(solution)/shard_map/mul | solution.py:541

commit v3 on v2

--- a/solution.py
+++ b/solution.py
@@ -41,11 +41,11 @@
 
 
 def kernel(
-    rm, cm, tl_in, tr_in, rl_in, rr_in, cl_in, cr_in, sk,
+    rm_in, cm_in, tl_in, tr_in, rl_in, rr_in, cl_in, cr_in, sk_in,
     outl, outr,
     RR, RL, CR, CL, WV, WS, CSP, BDh, BDl, CS, MX, S, SG, RT, RSP, RSM, RQP, RQM,
     TT, TLO, TRO, X, Q, WP, WW, BC, FSL, FSR, FRL, FRR,
-    ssem, rsem, lsem,
+    sk, rm, cm, ssem, rsem, lsem,
 ):
     d = lax.axis_index("depth")
     x = lax.axis_index("row")
@@ -95,6 +95,9 @@
         pltpu.make_async_copy(rl_in.at[pl.ds(2 * c, 2)], RL.at[y, :, pl.ds(4 * c, 4)], lsem.at[2]),
         pltpu.make_async_copy(cl_in, CL.at[x, :, pl.ds(4 * c, 4)], lsem.at[3]),
         pltpu.make_async_copy(tl_in.at[tile_i, tile_j], TLO, lsem.at[4]),
+        pltpu.make_async_copy(sk_in, sk, lsem.at[6]),
+        pltpu.make_async_copy(rm_in, rm, lsem.at[7]),
+        pltpu.make_async_copy(cm_in, cm, lsem.at[8]),
         pltpu.make_async_copy(tr_in.at[tile_i, tile_j], TRO, lsem.at[5]),
     ]
     for copy in local:
@@ -130,8 +133,12 @@
         recv(f"{t}-1{g}")
         send(f"{t}-f{g}", block(buf, chunk(y, 1), 1, g), block(buf, chunk(y, 1), 1, g), ydev(3))
 
-    def rows_end(t):
-        for came in ("+1c", "-0c", "+1o", "-0o", "+fc", "-fc", "+fo", "-fo"):
+    def rows_near(t):
+        for came in ("+1c", "-0c", "+1o", "-0o"):
+            recv(t + came)
+
+    def rows_far(t):
+        for came in ("+fc", "-fc", "+fo", "-fo"):
             recv(t + came)
 
     def cols_own(t, buf, of, src0, src1):
@@ -165,7 +172,9 @@
     send("Rs", cr_in, CR.at[x, :, pl.ds(4 * c, 4)], sib)
     rows_other("R", RR)
     send("Lsw", rl_in.at[pl.ds(2 * o, 2)], grp(RL, y, c), sib)
-    rows_own("L", RL, rl_in)
+
+    for copy in local:
+        copy.wait()
 
     of_lane = lax.broadcasted_iota(jnp.int32, (1, 256), 1) // K
     for q in range(8):
@@ -176,9 +185,6 @@
                 row = row + jnp.where(of_lane == kk, weight, 0.0)
             buf[q:q + 1, :] = row
     send("M", WS, WV.at[c], sib)
-    for copy in local:
-        copy.wait()
-
     def part_sketch(j, _):
         CSP[x, j] = dot_nt(
             sk[:, pl.ds(pl.multiple_of(CH * x, CH), CH)], CL[x, j, pl.ds(4 * c, 4)].reshape(256, CH)
@@ -190,6 +196,7 @@
     rows_on("R", RR, "c")
     cols_on("R", CR, half)
     rows_on("R", RR, "o")
+    rows_own("L", RL, rl_in)
     rows_other("L", RL)
     cols_to_sib("R", CR, early)
 
@@ -198,7 +205,8 @@
     TT[...] = own[0:K] + own[K:2 * K] + own[2 * K:]
 
     rows_on("L", RL, "c")
-    rows_end("R")
+    rows_near("R")
+    rows_far("R")
     cols_to_sib("R", CR, late)
     cols_on("C", CSP, part)
     cols_end("R")
@@ -237,7 +245,7 @@
     send("Ls", CL.at[x, :, pl.ds(4 * c, 4)], CL.at[x, :, pl.ds(4 * c, 4)], sib)
     recv("CS")
 
-    def mix_tile(q, _):
+    def mix_tile(q):
         j = lax.rem(q, 4)
         for g in range(2):
             both = CS[j, g]
@@ -246,54 +254,77 @@
             hi, lo = split2(mix)
             MX[q, 0:K, 256 * g:256 * (g + 1)] = hi
             MX[q, K:2 * K, 256 * g:256 * (g + 1)] = lo
-        return 0
-
-    lax.fori_loop(0, 8, mix_tile, 0)
-    rows_end("L")
-
-    def s_tile(q):
+
+    rows_near("L")
+
+    parts = (y, chunk(y, 3), chunk(y, 1), chunk(y, 2))
+
+    def s_tile(q, wave):
+        if wave[0] == 0:
+            mix_tile(q)
         i = lax.div(q, 4)
         both = MX[q]
-        for b in range(NX):
-            p = dot_nn(both, RL[b, i].reshape(512, CH))
-            S[q, :, CH * b:CH * (b + 1)] = p[0:K] + p[K:]
+        for n in range(*wave):
+            p = dot_nn(both, RL[parts[n], i].reshape(512, CH))
+            S[n, q] = p[0:K] + p[K:]
 
     def at(k):
         return lax.rem(z + k, NZ)
 
-    def sum_send(way, s, u):
+    def sum_send(wave, way, s, u):
         buf, dev, tile = (RSP, zdev(1), at(4 - s)) if way == "+" else (RSM, zdev(7), at(4 + s))
-        rows = slice(16 * u, 16 * u + 16)
+        ns, nd = slice(*wave), pl.ds(wave[0], wave[1] - wave[0])
         if s > 1 or (s == 1 and (u < 2) == (way == "+")):
-            recv(f"S{way}{s - 1}{u}")
-            S[tile, rows] += buf[s - 1, u]
-        send(f"S{way}{s}{u}", S.at[tile, pl.ds(16 * u, 16)], buf.at[s, u], dev)
-
-    s_tile(at(4))
-    for u in (0, 2, 1, 3):
-        sum_send("+" if u < 2 else "-", 0, u)
-    s_tile(at(3))
-    for u in (2, 3):
-        sum_send("+", 1, u)
-    s_tile(at(5))
-    for u in (0, 1):
-        sum_send("-", 1, u)
-    s_tile(at(2))
-    s_tile(at(6))
-    for u in (0, 1):
-        sum_send("+", 1, u)
-        sum_send("-", 1, u + 2)
-    s_tile(at(1))
-    s_tile(at(7))
+            recv(f"S{wave[0]}{way}{s - 1}{u}")
+            S[ns, tile, 16 * u:16 * u + 16] += buf[ns, s - 1, u]
+        send(f"S{wave[0]}{way}{s}{u}", S.at[nd, tile, pl.ds(16 * u, 16)], buf.at[nd, s, u], dev)
+
+    def sum_start(wave):
+        s_tile(at(4), wave)
+        for u in (0, 2, 1, 3):
+            sum_send(wave, "+" if u < 2 else "-", 0, u)
+        s_tile(at(3), wave)
+        for u in (2, 3):
+            sum_send(wave, "+", 1, u)
+        s_tile(at(5), wave)
+        for u in (0, 1):
+            sum_send(wave, "-", 1, u)
+
+    def sum_one(wave):
+        for u in (0, 1):
+            sum_send(wave, "+", 1, u)
+            sum_send(wave, "-", 1, u + 2)
+
+    def sum_two(wave):
+        for u, v in ((2, 0), (0, 2), (3, 1), (1, 3)):
+            sum_send(wave, "+", 2, u)
+            sum_send(wave, "-", 2, v)
+
+    def sum_three(wave):
+        for u in (0, 2, 1, 3):
+            sum_send(wave, "+", 3, u)
+            sum_send(wave, "-", 3, u)
+
+    near, opposite = (0, 3), (3, 4)
+    sum_start(near)
+    s_tile(at(2), near)
+    s_tile(at(6), near)
+    sum_one(near)
+    s_tile(at(1), near)
+    s_tile(at(7), near)
+    rows_far("L")
+    sum_start(opposite)
+    for k in (2, 6, 1, 7):
+        s_tile(at(k), opposite)
+    sum_one(opposite)
+    sum_two(near)
     cols_on("L", CL, half)
-    for u in (2, 3, 0, 1):
-        sum_send("+", 2, u)
-        sum_send("-", 2, (u + 2) % 4)
-    s_tile(z)
+    sum_two(opposite)
+    s_tile(z, near)
+    s_tile(z, opposite)
+    sum_three(near)
     cols_to_sib("L", CL, early)
-    for u in (2, 3, 0, 1):
-        sum_send("+", 3, u)
-        sum_send("-", 3, (u + 2) % 4)
+    sum_three(opposite)
     cols_to_sib("L", CL, late)
 
     def pass_on(s, u, way):
@@ -305,16 +336,20 @@
         send(f"G{way}{s}{u}", part_of, part_of, zdev(1 if way == "+" else 7))
 
     def pass_both(s, n):
-        pass_on(s, n, "+")
-        pass_on(s, (n + 2) % 4, "-")
+        pass_on(s, (0, 2, 1, 3)[n], "+")
+        pass_on(s, (2, 0, 3, 1)[n], "-")
 
     for u in (0, 2, 1, 3):
-        recv(f"S+3{u}")
-        recv(f"S-3{u}")
+        for wave in (near, opposite):
+            recv(f"S{wave[0]}+3{u}")
+            recv(f"S{wave[0]}-3{u}")
         rows = slice(16 * u, 16 * u + 16)
-        SG[z, rows] = (S[z, rows] + TT[rows]) + (RSP[3, u] + RSM[3, u])
-    for u in range(4):
-        pass_both(1, u)
+        for n in range(4):
+            cols = pl.ds(pl.multiple_of(CH * parts[n], CH), CH)
+            SG[z, rows, cols] = (S[n, z, rows] + TT[rows, cols]) + (RSP[n, 3, u] + RSM[n, 3, u])
+        if u >= 2:
+            pass_both(1, 2 * (u - 2))
+            pass_both(1, 2 * (u - 2) + 1)
 
     def tile_back(q):
         i = lax.div(q, 4)
@@ -396,7 +431,7 @@
     own = dot_nn(jnp.concatenate([h, m, l], axis=0), TRO[...])
     TT[...] = own[0:K] + own[K:2 * K] + own[2 * K:]
     pass_both(3, 3)
-    pass_both(4, 1)
+    pass_both(4, 2)
     tile_back(at(2))
     tile_back(at(6))
     for u in (2, 3):
@@ -472,31 +507,31 @@
             v = RT[q, rows_of(z)] + (RQP[3, u, q % 2] + RQM[3, u, q % 2])
             FSR[4 * q:4 * q + 4] = jnp.where(keep0, v[4:8], v[0:4])
             outr[2 * c + q // 4, q % 4] = jnp.where(keep0, v[0:4], v[4:8])
-    send("FR", FSR, FRR, sib)
+        send(f"FR{u}", FSR.at[pl.ds(8 * u, 8)], FRR.at[pl.ds(8 * u, 8)], sib)
     recv("FL")
     for q in range(8):
         outl[2 * o + q // 4, q % 4] = FRL[4 * q:4 * q + 4]
-    recv("FR")
-    for q in range(8):
-        outr[2 * o + q // 4, q % 4] = FRR[4 * q:4 * q + 4]
+    for u in range(4):
+        recv(f"FR{u}")
+        for q in (2 * u, 2 * u + 1):
+            outr[2 * o + q // 4, q % 4] = FRR[4 * q:4 * q + 4]
     for copy in descs.values():
         copy.wait_send()
 
 
-N_COPIES = 2 * (13 + 6 + 7) + 6 + 2 + 28 + 28 + 7 + 28 + 2
+N_COPIES = 2 * (13 + 6 + 7) + 6 + 2 + 56 + 28 + 7 + 28 + 5
 
 
 def on_device(
     tile_left, tile_right, row_left, row_right, col_left, col_right, row_mask, col_mask, sketch
 ):
     vmem = pl.BlockSpec(memory_space=pltpu.VMEM)
-    smem = pl.BlockSpec(memory_space=pltpu.SMEM)
     hbm = pl.BlockSpec(memory_space=pl.ANY)
     out = jax.ShapeDtypeStruct((4, 4, 4, NB), F32)
     basis, projection = pl.pallas_call(
         kernel,
         out_shape=(out, out),
-        in_specs=[smem, smem, hbm, hbm, hbm, hbm, hbm, hbm, vmem],
+        in_specs=[hbm] * 9,
         out_specs=(vmem, vmem),
         scratch_shapes=[
             pltpu.VMEM((NX, 2, 8, K, CH), BF16),
@@ -510,11 +545,11 @@
             pltpu.VMEM((8, 2, 256, 256), BF16),
             pltpu.VMEM((4, 2, 2 * K, 256), BF16),
             pltpu.VMEM((8, 2 * K, 512), BF16),
+            pltpu.VMEM((4, 8, K, CH), F32),
             pltpu.VMEM((8, K, NB), F32),
             pltpu.VMEM((8, K, NB), F32),
-            pltpu.VMEM((8, K, NB), F32),
-            pltpu.VMEM((4, 4, 16, NB), F32),
-            pltpu.VMEM((4, 4, 16, NB), F32),
+            pltpu.VMEM((4, 4, 4, 16, CH), F32),
+            pltpu.VMEM((4, 4, 4, 16, CH), F32),
             pltpu.VMEM((4, 4, 2, 8, NB), F32),
             pltpu.VMEM((4, 4, 2, 8, NB), F32),
             pltpu.VMEM((K, NB), F32),
@@ -529,9 +564,12 @@
             pltpu.VMEM((32, NB), F32),
             pltpu.VMEM((32, NB), F32),
             pltpu.VMEM((32, NB), F32),
+            pltpu.VMEM((K, NB), BF16),
+            pltpu.SMEM((4, 4), jnp.int32),
+            pltpu.SMEM((4, 4), jnp.int32),
             pltpu.SemaphoreType.DMA((N_COPIES,)),
             pltpu.SemaphoreType.DMA((N_COPIES,)),
-            pltpu.SemaphoreType.DMA((6,)),
+            pltpu.SemaphoreType.DMA((9,)),
         ],
         compiler_params=pltpu.CompilerParams(
             collective_id=0, has_side_effects=True, vmem_limit_bytes=56 * 1024 * 1024

time: 124 us -> 122 us (0.984)
  Pallas kernels: 122 us -> 119 us
    pallas_call x1, Pallas kernels: 122 us -> 119 us  [on_device(): pl.pallas_call(kernel, out_shape=(out, out), in_specs=[hbm] * 9, out_spec...]
where the time goes in v3:
time: 122 us
  Pallas kernels  119 us (98%)
  other arithmetic  1.99 us (2%)
    pallas_call x1, Pallas kernels, on_device(): pl.pallas_call(kernel, out_shape=(out, out), in_specs=[hbm] * 9, out_spec...  119 us

profile of v3, /device:TPU:1, one launch (start us, length us, event | category | flops | bytes accessed | tf_op | source)
XLA Modules:
  0.0 122.0 jit_solution(12422107131273768645)
XLA Ops:
  0.6 119.3 %trailing_update.1 = (f32[4,4,4,1024]{3,2,1,0:T(4,128)}, f32[4,4,4,1024]{3,2,1,0:T(4,128)}) custom-call(s32[4,4]{1,0:T(4,128)} %rm_in.1, s32[4,4]{1,0:T(4,128)} %cm_in.1, bf16[4,4,64,1024]{3,2,1,0:T(8,128)(2,1)} %tl_in.1, bf16[4,4,64,1024]{3,2,1,0:T(8,128)(2,1)} %tr_in.1, bf16[4,4,64,256]{3,2,1,0:T(8,128)(2,1)} %rl_in.1, bf16[4,4,64,256]{3,2,1,0:T(8,128)(2,1)} %rr_in.1, ...), custom_call_target="tpu_custom_call" | custom-call | tf_op jit(solution)/shard_map/trailing_update/pallas_call | solution.py:531
  120.0 2.0 %broadcast_multiply_fusion = (f32[4,4,4,1024]{3,2,1,0:T(4,128)}, f32[4,4,4,1024]{3,2,1,0:T(4,128)}) fusion(f32[4,4,4,1024]{3,2,1,0:T(4,128)} %get-tuple-element.5, f32[4,4,4,1024]{3,2,1,0:T(4,128)} %get-tuple-element.4), kind=kLoop, calls=%fused_computation | loop fusion | flops 131072 | bytes 1048576 | tf_op jit(solution)/shard_map/mul | solution.py:579
